TPU v7x, 32 devices: a whole 2x2x4 slice. The times are simulated.
32 devices in a mesh: seq: 16 (over z, y, x), chan: 2 (over core).
Axes of the slice: x: 2, y: 2, z: 4, core: 2. Of those that a mesh axis runs over, the one named last changes fastest.
Arguments:
- query_proj: bfloat16 [2048, 2048], P('seq', 'chan'), may hold values from -70 to 70
- key_proj: bfloat16 [2048, 2048], P('seq', 'chan'), may hold values from -6 to 6
- value_proj: bfloat16 [2048, 2048], P('seq', 'chan'), may hold values from -6 to 6
- long_filter: float32 [2048, 2048], P('seq', 'chan'), may hold values from -0.125 to 0.125
- skip_gain: float32 [2048], P('chan'), may hold values from -1 to 1
- norm_gain: float32 [2048], P('chan'), may hold values from 0.25 to 1.75
- out_grad: bfloat16 [2048, 2048], P('seq', 'chan'), may hold values from -6 to 6
Outputs:
- block_out: bfloat16 [2048, 2048], P('seq', 'chan')
- query_grad: bfloat16 [2048, 2048], P('seq', 'chan')
- key_grad: bfloat16 [2048, 2048], P('seq', 'chan')
- value_grad: bfloat16 [2048, 2048], P('seq', 'chan')
- filter_grad: float32 [2048, 2048], P('seq', 'chan')
All inputs are finite; a program needn't handle non-finite values.
Results may differ from a plain program's by a relative error of at most 0.0055.
Values sent between devices are 32-bit elements; how exact they have to be, the bound alone decides.
A program may use at most 128 MiB of HBM per device.

v0:
```python
import math

import jax
import jax.numpy as jnp
from jax import lax
from jax.sharding import PartitionSpec as P

exact_mode = lax.Precision.HIGHEST
epsilon_value = 1e-05


def dft_matrix(count, sign):
    indices = jnp.arange(count, dtype=jnp.int32)
    product = indices[:, None] * indices[None, :] % count
    angles = product.astype(jnp.float32) * (2.0 * math.pi / count)
    cosine = jnp.cos(angles)
    sine_part = sign * jnp.sin(angles)
    return jnp.stack([jnp.stack([cosine, -sine_part], 1), jnp.stack([sine_part, cosine], 1)], 0)


def rotate(field, angles):
    cos_part = jnp.cos(angles)
    sin_part = jnp.sin(angles)
    real_part = field[:, 0]
    imag_part = field[:, 1]
    return jnp.stack(
        [real_part * cos_part - imag_part * sin_part, real_part * sin_part + imag_part * cos_part],
        1,
    )


def prepare(signals, positions, length):
    angles = (positions.astype(jnp.float32) * (-math.pi / length))[..., None]
    cos_part = jnp.cos(angles)
    sin_part = jnp.sin(angles)
    real_in = signals[:, 0]
    real_part = jnp.stack([real_in, real_in * cos_part], 1)
    imag_part = jnp.stack([jnp.zeros_like(real_in), real_in * sin_part], 1)
    return jnp.stack([real_part, imag_part], 1)


def finish(field, positions, length):
    angles = (positions.astype(jnp.float32) * (math.pi / length))[..., None]
    second = rotate(field[:, :, 1], angles)
    return (field[:, :, 0] + second) / (2.0 * length)


def complex_product(first, second, conjugate):
    second_imag = -second[1] if conjugate else second[1]
    return jnp.stack(
        [
            first[0] * second[0] - first[1] * second_imag,
            first[0] * second_imag + first[1] * second[0],
        ],
        0,
    )


def body(query_proj, key_proj, value_proj, long_filter, skip_gain, norm_gain, out_grad):
    tok_rows, chan_width = query_proj.shape
    seq_count = lax.axis_size("seq")
    seq_index = lax.axis_index("seq")
    length = tok_rows * seq_count
    channel_total = chan_width * lax.axis_size("chan")
    narrow_rows = tok_rows // seq_count
    forward_rows = dft_matrix(tok_rows, -1.0)
    inverse_rows = dft_matrix(tok_rows, 1.0)

    def block_places():
        offsets = seq_index * narrow_rows + jnp.arange(narrow_rows, dtype=jnp.int32)
        return jnp.arange(seq_count, dtype=jnp.int32)[:, None] * tok_rows + offsets[None, :]

    def channel_forward(signals):
        batch, width = (signals.shape[0], signals.shape[1])
        blocks = signals.reshape(batch, width, seq_count, narrow_rows, chan_width)
        spread = lax.all_to_all(blocks, "seq", split_axis=2, concat_axis=2, tiled=True)
        field = prepare(spread, block_places(), length)
        field = jnp.einsum(
            "pkqn,bqsnjc->bpskjc", dft_matrix(seq_count, -1.0), field, precision=exact_mode
        )
        offsets = seq_index * narrow_rows + jnp.arange(narrow_rows, dtype=jnp.int32)
        turns = jnp.arange(seq_count, dtype=jnp.int32)[:, None] * offsets[None, :] % length
        field = rotate(field, (turns.astype(jnp.float32) * (-2.0 * math.pi / length))[:, :, None])
        field = lax.all_to_all(field, "seq", split_axis=3, concat_axis=3, tiled=True)
        field = field.reshape(batch, 2, 2, tok_rows, chan_width)
        return jnp.einsum("pkqr,bqsrc->bpskc", forward_rows, field, precision=exact_mode)

    def channel_inverse(spectra, parts):
        batch = spectra.shape[0]
        field = jnp.einsum("pkqr,bqsrc->bpskc", inverse_rows, spectra, precision=exact_mode)
        turns = seq_index * jnp.arange(tok_rows, dtype=jnp.int32) % length
        field = rotate(field, (turns.astype(jnp.float32) * (2.0 * math.pi / length))[:, None])
        field = field.reshape(batch, 2, 2, seq_count, narrow_rows, chan_width)
        field = lax.all_to_all(field, "seq", split_axis=3, concat_axis=3, tiled=True)
        field = jnp.einsum(
            "pkqn,bqsnjc->bpskjc", dft_matrix(seq_count, 1.0), field, precision=exact_mode
        )
        result = finish(field, block_places(), length)[:, :parts]
        result = lax.all_to_all(result, "seq", split_axis=2, concat_axis=2, tiled=True)
        return result.reshape(batch, parts, tok_rows, chan_width)

    def transform(signals):
        return channel_forward(signals)

    def untransform(spectra, parts):
        return channel_inverse(spectra, parts)

    queries = query_proj.astype(jnp.float32)
    key_rows = key_proj.astype(jnp.float32)
    values = value_proj.astype(jnp.float32)
    gated_in = key_rows * values
    spectra = transform(jnp.stack([gated_in, long_filter], 0)[:, None])
    gated_spec = spectra[0]
    filter_spec = spectra[1]
    mixed_spec = complex_product(gated_spec, filter_spec, False)
    convolved = untransform(mixed_spec[None], 1)[0, 0]
    mixed = convolved + skip_gain[None, :] * gated_in
    activated = queries * mixed
    squares = lax.psum(jnp.sum(activated * activated, axis=1), "chan")
    inverse_rms = lax.rsqrt(squares / channel_total + epsilon_value)[:, None]
    block_out = (activated * inverse_rms * norm_gain[None, :]).astype(jnp.bfloat16)
    scaled_grad = out_grad.astype(jnp.float32) * norm_gain[None, :]
    cross_sum = lax.psum(jnp.sum(scaled_grad * activated, axis=1), "chan")
    cross_mean = (cross_sum / channel_total)[:, None]
    act_grad = inverse_rms * scaled_grad - activated * inverse_rms**3 * cross_mean
    query_grad = (act_grad * mixed).astype(jnp.bfloat16)
    mix_grad = act_grad * queries
    grad_spec = transform(mix_grad[None, None])[0]
    toward_input = complex_product(grad_spec, filter_spec, True)
    toward_filter = complex_product(grad_spec, gated_spec, True)
    results = untransform(jnp.stack([toward_input, toward_filter], 0), 1)
    input_part = results[0, 0]
    filter_grad = results[1, 0]
    gated_grad = input_part + skip_gain[None, :] * mix_grad
    key_grad = (gated_grad * values).astype(jnp.bfloat16)
    value_grad = (gated_grad * key_rows).astype(jnp.bfloat16)
    return (block_out, query_grad, key_grad, value_grad, filter_grad)


def solution(mesh):
    return jax.shard_map(
        body,
        mesh=mesh,
        in_specs=(
            P("seq", "chan"),
            P("seq", "chan"),
            P("seq", "chan"),
            P("seq", "chan"),
            P("chan"),
            P("chan"),
            P("seq", "chan"),
        ),
        out_specs=(
            P("seq", "chan"),
            P("seq", "chan"),
            P("seq", "chan"),
            P("seq", "chan"),
            P("seq", "chan"),
        ),
        check_vma=False,
    )
```

profile of v0, /device:TPU:0, one launch (start us, length us, event | category | flops | bytes accessed | tf_op | source)
XLA Modules:
  0.0 479.8 jit_solution(17799157703883698756)
XLA Ops:
  0.6 1.1 fusion.45
  1.7 1.1 pad_maximum_fusion.5
  2.9 1.1 copy.48
  4.0 8.3 %all-to-all-start = ((f32[2,1,16,8,1024]{4,3,1,0,2:T(8,128)}), f32[2,1,16,8,1024]{4,3,1,0,2:T(8,128)S(1)}, u32[]{:S(2)}, u32[]{:S(2)}) async-start(f32[2,1,16,8,1024]{4,3,1,0,2:T(8,128)} %copy.48), calls=%async_computation | async-start | bytes 2097152 | tf_op jit(solution)/shard_map/all_to_all | solution.py:76
  12.7 24.1 %all-to-all-done = f32[2,1,16,8,1024]{4,3,1,0,2:T(8,128)S(1)} async-done(((f32[2,1,16,8,1024]{4,3,1,0,2:T(8,128)}), f32[2,1,16,8,1024]{4,3,1,0,2:T(8,128)S(1)}, u32[]{:S(2)}, u32[]{:S(2)}) %all-to-all-start) | async-done | bytes 1048608 | tf_op jit(solution)/shard_map/all_to_all | solution.py:76
  37.8 5.5 %fusion.18 = f32[2,2,2,16,8,1024]{5,3,1,4,2,0:T(8,128)S(1)} fusion(f32[2,1,2,16,8,1024]{5,3,1,4,2,0:T(8,128)S(1)} %get-tuple-element.63, f32[2,1,2,16,8,1024]{5,3,1,4,2,0:T(8,128)S(1)} %get-tuple-element.62, f32[1,16,2,16]{3,1,2,0:T(8,128)S(1)} %get-tuple-element.50, f32[1,16,2,16]{3,1,2,0:T(8,128)S(1)} %get-tuple-element.51), kind=kOutput, calls=%fused_computation.17 | convolution fusion | flops 403702784 | bytes 8392704 | tf_op jit(solution)/shard_map/pkqn,bqsnjc->bpskjc/dot_general | solution.py:78
  44.9 5.3 %copy.52 = f32[2,2,2,16,8,1024]{5,1,4,2,0,3:T(2,128)} copy(f32[2,2,2,16,8,1024]{5,3,1,4,2,0:T(8,128)S(1)} %pad_maximum_fusion) | data formatting | bytes 8388608 | tf_op jit(solution)/shard_map/stack | solution.py:26
  50.2 6.1 %all-to-all-start.1 = ((f32[2,2,2,16,8,1024]{5,1,4,2,0,3:T(2,128)}), f32[2,2,2,16,8,1024]{5,1,4,2,0,3:T(2,128)}, u32[]{:S(2)}, u32[]{:S(2)}) async-start(f32[2,2,2,16,8,1024]{5,1,4,2,0,3:T(2,128)} %copy.52), calls=%async_computation.1 | async-start | bytes 8388608 | tf_op jit(solution)/shard_map/all_to_all | solution.py:84
  57.2 77.0 %all-to-all-done.1 = f32[2,2,2,16,8,1024]{5,1,4,2,0,3:T(2,128)} async-done(((f32[2,2,2,16,8,1024]{5,1,4,2,0,3:T(2,128)}), f32[2,2,2,16,8,1024]{5,1,4,2,0,3:T(2,128)}, u32[]{:S(2)}, u32[]{:S(2)}) %all-to-all-start.1) | async-done | bytes 4194336 | tf_op jit(solution)/shard_map/all_to_all | solution.py:84
  134.2 9.3 %fusion.9 = f32[2,2,2,128,1024]{3,4,1,2,0:T(8,128)S(1)} fusion(f32[1,128,2,128]{3,1,2,0:T(8,128)S(1)} %get-tuple-element.46, f32[1,128,2,128]{3,1,2,0:T(8,128)S(1)} %get-tuple-element.47, f32[2,2,2,16,8,1024]{5,1,4,2,0,3:T(2,128)} %all-to-all-done.1), kind=kOutput, calls=%fused_computation.14 | convolution fusion | flops 3221291008 | bytes 8650752 | tf_op jit(solution)/shard_map/pkqr,bqsrc->bpskc/dot_general | solution.py:86
  143.8 1.7 copy-done
  145.5 2.0 fusion.34
  147.9 1.1 copy.59
  150.1 2.0 pad_maximum_fusion.2
  152.1 66.7 %all_to_all.40 = f32[1,2,2,16,8,1024]{5,1,4,2,0,3:T(2,128)S(1)} all-to-all(f32[1,2,2,16,8,1024]{5,1,4,2,0,3:T(2,128)S(1)} %pad_maximum_fusion.2), channel_id=1, replica_groups=mesh['seq'=16,'chan'=2] {'seq'}, dimensions={3} | all-to-all | bytes 4194304 | tf_op jit(solution)/shard_map/all_to_all | solution.py:94
  218.9 3.5 fusion.30
  223.6 17.9 %all_to_all.41 = f32[1,1,16,8,1024]{4,1,3,0,2:T(1,128)S(1)} all-to-all(f32[1,1,16,8,1024]{4,1,3,0,2:T(1,128)S(1)} %copy.62), channel_id=1, replica_groups=mesh['seq'=16,'chan'=2] {'seq'}, dimensions={2} | all-to-all | bytes 1048576 | tf_op jit(solution)/shard_map/all_to_all | solution.py:99
  241.9 2.5 all-reduce.2
  244.7 19.1 %all_to_all.42 = f32[1,1,16,8,1024]{4,3,1,0,2:T(8,128)S(1)} all-to-all(f32[1,1,16,8,1024]{4,3,1,0,2:T(8,128)S(1)} %fusion.46), channel_id=1, replica_groups=mesh['seq'=16,'chan'=2] {'seq'}, dimensions={2} | all-to-all | bytes 1048576 | tf_op jit(solution)/shard_map/all_to_all | solution.py:76
  264.2 2.1 fusion.33
  267.1 1.6 copy.67
  268.7 52.0 %all_to_all.43 = f32[1,2,2,16,8,1024]{5,1,4,2,0,3:T(2,128)S(1)} all-to-all(f32[1,2,2,16,8,1024]{5,1,4,2,0,3:T(2,128)S(1)} %copy.67), channel_id=1, replica_groups=mesh['seq'=16,'chan'=2] {'seq'}, dimensions={3} | all-to-all | bytes 4194304 | tf_op jit(solution)/shard_map/all_to_all | solution.py:84
  320.7 3.8 fusion.37
  325.3 3.9 fusion.12
  329.9 2.2 copy.72
  332.1 2.4 copy.73
  334.4 4.2 pad_maximum_fusion.1
  338.6 96.9 %all_to_all.44 = f32[2,2,2,16,8,1024]{5,1,4,2,0,3:T(2,128)S(1)} all-to-all(f32[2,2,2,16,8,1024]{5,1,4,2,0,3:T(2,128)S(1)} %pad_maximum_fusion.1), channel_id=1, replica_groups=mesh['seq'=16,'chan'=2] {'seq'}, dimensions={3} | all-to-all | bytes 8388608 | tf_op jit(solution)/shard_map/all_to_all | solution.py:94
  435.5 8.3 %fusion.15 = f32[2,2,2,16,8,1024]{5,3,1,4,2,0:T(8,128)S(1)} fusion(f32[2,2,2,16,8,1024,1]{5,1,4,2,0,3,6:T(2,128)S(1)} %bitcast.260, f32[1,16,2,16]{3,1,2,0:T(8,128)S(1)} %get-tuple-element.49, f32[1,16,2,16]{3,1,2,0:T(8,128)S(1)} %get-tuple-element.48), kind=kOutput, calls=%fused_computation.16 | convolution fusion | flops 402654208 | bytes 8392704 | tf_op jit(solution)/shard_map/pkqn,bqsnjc->bpskjc/dot_general | solution.py:95
  446.0 29.2 %all_to_all.45 = f32[2,1,16,8,1024]{4,1,3,0,2:T(1,128)S(1)} all-to-all(f32[2,1,16,8,1024]{4,1,3,0,2:T(1,128)S(1)} %copy.76), channel_id=1, replica_groups=mesh['seq'=16,'chan'=2] {'seq'}, dimensions={2} | all-to-all | bytes 2097152 | tf_op jit(solution)/shard_map/all_to_all | solution.py:99
  475.2 1.1 fusion.109
  477.2 1.4 fusion.41
  (57 shorter events, 13.7 us)
Async XLA Ops:
  4.0 32.8 %all-to-all-start = ((f32[2,1,16,8,1024]{4,3,1,0,2:T(8,128)}), f32[2,1,16,8,1024]{4,3,1,0,2:T(8,128)S(1)}, u32[]{:S(2)}, u32[]{:S(2)}) async-start(f32[2,1,16,8,1024]{4,3,1,0,2:T(8,128)} %copy.48), calls=%async_computation | async-start | bytes 2097152 | tf_op jit(solution)/shard_map/all_to_all | solution.py:76
  50.2 84.0 %all-to-all-start.1 = ((f32[2,2,2,16,8,1024]{5,1,4,2,0,3:T(2,128)}), f32[2,2,2,16,8,1024]{5,1,4,2,0,3:T(2,128)}, u32[]{:S(2)}, u32[]{:S(2)}) async-start(f32[2,2,2,16,8,1024]{5,1,4,2,0,3:T(2,128)} %copy.52), calls=%async_computation.1 | async-start | bytes 8388608 | tf_op jit(solution)/shard_map/all_to_all | solution.py:84
  143.6 2.0 copy-start
  222.9 18.7 %copy-start.2 = (bf16[128,1024]{1,0:T(8,128)(2,1)S(1)}, bf16[128,1024]{1,0:T(8,128)(2,1)}, u32[]{:S(2)}) copy-start(bf16[128,1024]{1,0:T(8,128)(2,1)} %param.13) | copy-start | bytes 786436
  222.9 18.6 %copy-start.3 = (bf16[128,1024]{1,0:T(8,128)(2,1)S(1)}, bf16[128,1024]{1,0:T(8,128)(2,1)}, u32[]{:S(2)}) copy-start(bf16[128,1024]{1,0:T(8,128)(2,1)} %param.7) | copy-start | bytes 786436
  222.9 18.6 %copy-start.4 = (bf16[128,1024]{1,0:T(8,128)(2,1)S(1)}, bf16[128,1024]{1,0:T(8,128)(2,1)}, u32[]{:S(2)}) copy-start(bf16[128,1024]{1,0:T(8,128)(2,1)} %param.8) | copy-start | bytes 786436
  222.9 18.6 %copy-start.5 = (bf16[128,1024]{1,0:T(8,128)(2,1)S(1)}, bf16[128,1024]{1,0:T(8,128)(2,1)}, u32[]{:S(2)}) copy-start(bf16[128,1024]{1,0:T(8,128)(2,1)} %param.9) | copy-start | bytes 786436
  222.9 18.6 %copy-start.6 = (f32[1024]{0:T(1024)S(1)}, f32[1024]{0:T(1024)}, u32[]{:S(2)}) copy-start(f32[1024]{0:T(1024)} %param.12) | copy-start | bytes 12292
  222.9 18.6 %copy-start.7 = (f32[1024]{0:T(1024)S(1)}, f32[1024]{0:T(1024)}, u32[]{:S(2)}) copy-start(f32[1024]{0:T(1024)} %param.11) | copy-start | bytes 12292
  320.6 3.9 copy-start.1
where the time goes:
time: 488 us; the launch traced here: 480 us
  blocking collectives  284 us (58%)
  waiting for transfers between devices  101 us (21%)
  matrix products  38.5 us (8%)
  local copies, waits for them, and re-layouts  21 us (4%)
  other arithmetic  19.1 us (4%)
  starting transfers between devices  14.4 us (3%)
    all_to_all x2, blocking collectives, channel_inverse(): lax.all_to_all(field, 'seq', split_axis=3, concat_axis=3, tiled=True)  164 us
    all_to_all x1, waiting for transfers between devices, channel_forward(): lax.all_to_all(field, 'seq', split_axis=3, concat_axis=3, tiled=True)  77 us
    all_to_all x1, blocking collectives, channel_forward(): lax.all_to_all(field, 'seq', split_axis=3, concat_axis=3, tiled=True)  52 us
    all_to_all x2, blocking collectives, channel_inverse(): lax.all_to_all(result, 'seq', split_axis=2, concat_axis=2, tiled=True)  47.1 us
    all_to_all x1, waiting for transfers between devices, channel_forward(): lax.all_to_all(blocks, 'seq', split_axis=2, concat_axis=2, tiled=True)  24.1 us
    all_to_all x1, blocking collectives, channel_forward(): lax.all_to_all(blocks, 'seq', split_axis=2, concat_axis=2, tiled=True)  19.1 us
    another operation x6, local copies, waits for them, and re-layouts, rotate(): jnp.stack([real_part * cos_part - imag_part * sin_part, real_part * sin_p...  13.6 us
    dot_general x2, matrix products, channel_forward(): jnp.einsum('pkqr,bqsrc->bpskc', forward_rows, field, precision=exact_mode)  13.2 us
  transfers between devices with their start and end apart: 2, of which 2 were waited for; matrix products, arithmetic and copies ran while one was open for 0% of the time, Pallas kernels for 0%

commit v1 on v0

--- a/solution.py
+++ b/solution.py
@@ -1,8 +1,12 @@
+import functools
 import math
 
 import jax
 import jax.numpy as jnp
+import numpy as np
 from jax import lax
+from jax.experimental import pallas as pl
+from jax.experimental.pallas import tpu as pltpu
 from jax.sharding import PartitionSpec as P
 
 exact_mode = lax.Precision.HIGHEST
@@ -56,7 +60,7 @@
     )
 
 
-def body(query_proj, key_proj, value_proj, long_filter, skip_gain, norm_gain, out_grad):
+def wide_body(query_proj, key_proj, value_proj, long_filter, skip_gain, norm_gain, out_grad):
     tok_rows, chan_width = query_proj.shape
     seq_count = lax.axis_size("seq")
     seq_index = lax.axis_index("seq")
@@ -137,9 +141,377 @@
     return (block_out, query_grad, key_grad, value_grad, filter_grad)
 
 
+MESH = pl.DeviceIdType.MESH
+GATED, FILTER, CONV, MIXGRAD, INPUT, FGRAD = range(6)
+
+
+def split_matrix(matrix):
+    matrix = jnp.asarray(matrix, jnp.float32)
+    high = matrix.astype(jnp.bfloat16)
+    low = (matrix - high.astype(jnp.float32)).astype(jnp.bfloat16)
+    return jnp.concatenate([high, low, high], 1)
+
+
+def block_matrices(rows):
+    freqs = 2 * np.arange(rows) + 1
+    places = np.arange(2 * rows)
+    angles = np.pi / (2 * rows) * (freqs[:, None] * places[None, :] % (4 * rows))
+    forward = np.concatenate([np.cos(angles), -np.sin(angles)], 0)[:, :rows]
+    inverse = np.concatenate([np.cos(angles), -np.sin(angles)], 0).T / rows
+    return split_matrix(forward), split_matrix(inverse)
+
+
+def split_dot(matrix, values):
+    high = values.astype(jnp.bfloat16)
+    low = (values - high.astype(jnp.float32)).astype(jnp.bfloat16)
+    return jnp.dot(
+        matrix, jnp.concatenate([high, high, low], 0), preferred_element_type=jnp.float32
+    )
+
+
+def fast_kernel(
+    seq_count,
+    q_ref, k_ref, v_ref, f_ref, skip_ref, norm_ref, g_ref, fwd_ref, inv_ref,
+    out_ref, qg_ref, kg_ref, vg_ref, fg_ref,
+    send, recv, h_spec, h_swap, x_spec, x_swap, m_spec, m_swap, z_spec, fields,
+    mixed_ref, mix_ref, stat_send, stat_recv,
+    send_sems, recv_sems, stat_sems,
+):
+    rows, width = q_ref.shape
+    half = rows // 2
+    pairs = seq_count // 2
+    channel_total = 2 * width
+    me = lax.axis_index("seq")
+    core = lax.axis_index("chan")
+    f32 = jnp.float32
+
+    barrier = pltpu.get_barrier_semaphore()
+
+    def greet(step, carry):
+        peer = lax.rem(me + step, seq_count)
+        pl.semaphore_signal(barrier, inc=1, device_id={"seq": peer}, device_id_type=MESH)
+        return carry
+
+    lax.fori_loop(1, seq_count, greet, 0)
+    pl.semaphore_signal(barrier, inc=1, device_id={"chan": 1 - core}, device_id_type=MESH)
+
+    def first_lanes(count):
+        return lax.broadcasted_iota(jnp.int32, (count, 128), 1) < 64
+
+    def swap(values):
+        return pltpu.roll(values, 64, 1)
+
+    def lanes(tile):
+        return pl.ds(pl.multiple_of(tile * 128, 128), 128)
+
+    def pack(unit, tile, values):
+        top, bottom = values[:half], values[half:]
+        left = first_lanes(half)
+        send[unit, 2 * tile] = jnp.where(left, top, swap(bottom))
+        send[unit, 2 * tile + 1] = jnp.where(left, swap(top), bottom)
+
+    def unpack(unit, tile):
+        first, second = recv[unit, 2 * tile], recv[unit, 2 * tile + 1]
+        left = first_lanes(half)
+        return jnp.concatenate(
+            [jnp.where(left, first, swap(second)), jnp.where(left, swap(first), second)], 0
+        )
+
+    def remote(unit, src, dst, peer, send_slot, recv_slot):
+        return pltpu.make_async_remote_copy(
+            src_ref=send.at[unit, src],
+            dst_ref=recv.at[unit, dst],
+            send_sem=send_sems.at[unit, send_slot],
+            recv_sem=recv_sems.at[unit, recv_slot],
+            device_id={"seq": peer},
+            device_id_type=MESH,
+        )
+
+    def send_all(unit):
+        def one(step, carry):
+            peer = lax.rem(me + step, seq_count)
+            remote(unit, peer, me, peer, peer, me).start()
+            return carry
+
+        lax.fori_loop(1, seq_count, one, 0)
+        recv[unit, me] = send[unit, me]
+
+    def receive_all(unit):
+        def one(step, carry):
+            peer = lax.rem(me + seq_count - step, seq_count)
+            remote(unit, peer, peer, peer, peer, peer).wait_recv()
+            return carry
+
+        lax.fori_loop(1, seq_count, one, 0)
+
+    def sent_all(unit):
+        def one(step, carry):
+            peer = lax.rem(me + step, seq_count)
+            remote(unit, peer, me, peer, peer, me).wait_send()
+            return carry
+
+        lax.fori_loop(1, seq_count, one, 0)
+
+    def spectrum(unit, spec, swapped):
+        def one(step, carry):
+            block = jnp.concatenate([unpack(unit, 2 * step), unpack(unit, 2 * step + 1)], 1)
+            field = split_dot(fwd_ref[...], block)
+            for side in range(2):
+                part = field[:, 128 * side:128 * side + 128]
+                spec[2 * step + side] = part
+                swapped[2 * step + side] = swap(part)
+            return carry
+
+        lax.fori_loop(0, pairs // 2, one, 0)
+
+    def load(ref, tile, count):
+        first = pl.multiple_of(tile * 8, 8)
+        real = [ref[k, pl.ds(first, 8), :] for k in range(count)]
+        imag = [ref[k, pl.ds(first + rows, 8), :] for k in range(count)]
+        return real, imag
+
+    def convolve():
+        def one(tile, carry):
+            left = first_lanes(8)
+            zero = jnp.zeros((8, 128), f32)
+            hr, hi = load(h_spec, tile, pairs)
+            sr, si = load(h_swap, tile, pairs)
+            xr, xi = load(x_spec, tile, pairs)
+            yr, yi = load(x_swap, tile, pairs)
+            even = [
+                (jnp.where(left, hr[k], sr[k]), jnp.where(left, hi[k], si[k]))
+                for k in range(pairs)
+            ]
+            odd = [
+                (
+                    jnp.where(left, sr[k - 1] if k else zero, hr[k]),
+                    jnp.where(left, si[k - 1] if k else zero, hi[k]),
+                )
+                for k in range(pairs)
+            ]
+            first = pl.multiple_of(tile * 8, 8)
+            for n in range(pairs):
+                real, imag = zero, zero
+                for k in range(n + 1):
+                    er, ei = even[k]
+                    tr, ti = odd[k]
+                    m = n - k
+                    real = real + (xr[m] * er - xi[m] * ei) + (yr[m] * tr - yi[m] * ti)
+                    imag = imag + (xr[m] * ei + xi[m] * er) + (yr[m] * ti + yi[m] * tr)
+                z_spec[n, pl.ds(first, 8), :] = real
+                z_spec[n, pl.ds(first + rows, 8), :] = imag
+            return carry
+
+        lax.fori_loop(0, rows // 8, one, 0)
+
+    def correlate(spec, swapped):
+        def one(tile, carry):
+            left = first_lanes(8)
+            zero = jnp.zeros((8, 128), f32)
+            hr, hi = load(spec, tile, pairs)
+            sr, si = load(swapped, tile, pairs)
+            xr, xi = load(m_spec, tile, pairs)
+            yr, yi = load(m_swap, tile, pairs)
+            even = [
+                (jnp.where(left, hr[k], sr[k]), jnp.where(left, hi[k], si[k]))
+                for k in range(pairs)
+            ]
+            odd = [
+                (
+                    jnp.where(left, sr[k], hr[k - 1] if k else zero),
+                    jnp.where(left, si[k], hi[k - 1] if k else zero),
+                )
+                for k in range(pairs)
+            ]
+            first = pl.multiple_of(tile * 8, 8)
+            for n in range(pairs):
+                real, imag = zero, zero
+                for k in range(pairs - n):
+                    er, ei = even[k]
+                    tr, ti = odd[k]
+                    m = n + k
+                    real = real + (xr[m] * er + xi[m] * ei) + (yr[m] * tr + yi[m] * ti)
+                    imag = imag + (xi[m] * er - xr[m] * ei) + (yi[m] * tr - yr[m] * ti)
+                z_spec[n, pl.ds(first, 8), :] = real
+                z_spec[n, pl.ds(first + rows, 8), :] = imag
+            return carry
+
+        lax.fori_loop(0, rows // 8, one, 0)
+
+    def invert(unit, forward):
+        def one(step, carry):
+            block = jnp.concatenate([z_spec[2 * step], z_spec[2 * step + 1]], 1)
+            field = split_dot(inv_ref[...], block)
+            fields[2 * step + 1] = field[:, :128]
+            fields[2 * step + 2] = field[:, 128:]
+            return carry
+
+        lax.fori_loop(0, pairs // 2, one, 0)
+
+        def join(tile, carry):
+            left = first_lanes(rows)
+            here = swap(fields[tile + 1, rows:, :])
+            if forward:
+                there = swap(fields[tile, rows:, :])
+                result = fields[tile + 1, :rows, :] + jnp.where(left, there, here)
+            else:
+                there = swap(fields[tile + 2, rows:, :])
+                result = fields[tile + 1, :rows, :] - jnp.where(left, here, there)
+            pack(unit, tile, result)
+            return carry
+
+        lax.fori_loop(0, pairs, join, 0)
+
+    def pack_inputs(tile, carry):
+        at = lanes(tile)
+        pack(FILTER, tile, f_ref[:, at])
+        pack(GATED, tile, k_ref[:, at].astype(f32) * v_ref[:, at].astype(f32))
+        return carry
+
+    lax.fori_loop(0, pairs, pack_inputs, 0)
+    fields[0] = jnp.zeros((2 * rows, 128), f32)
+    fields[pairs + 1] = jnp.zeros((2 * rows, 128), f32)
+
+    pl.semaphore_wait(barrier, seq_count)
+    send_all(FILTER)
+    send_all(GATED)
+    receive_all(FILTER)
+    spectrum(FILTER, h_spec, h_swap)
+    receive_all(GATED)
+    spectrum(GATED, x_spec, x_swap)
+    convolve()
+    invert(CONV, True)
+    send_all(CONV)
+    receive_all(CONV)
+
+    def activate(tile, carry):
+        squares, crosses = carry
+        at = lanes(tile)
+        gated = k_ref[:, at].astype(f32) * v_ref[:, at].astype(f32)
+        mixed = unpack(CONV, tile) + skip_ref[:, at] * gated
+        mixed_ref[tile] = mixed
+        activated = q_ref[:, at].astype(f32) * mixed
+        scaled = g_ref[:, at].astype(f32) * norm_ref[:, at]
+        return squares + activated * activated, crosses + scaled * activated
+
+    nothing = jnp.zeros((rows, 128), f32)
+    squares, crosses = lax.fori_loop(0, pairs, activate, (nothing, nothing))
+    stat_send[0] = jnp.broadcast_to(jnp.sum(squares, axis=1, keepdims=True), (rows, 128))
+    stat_send[1] = jnp.broadcast_to(jnp.sum(crosses, axis=1, keepdims=True), (rows, 128))
+    stats = pltpu.make_async_remote_copy(
+        src_ref=stat_send,
+        dst_ref=stat_recv,
+        send_sem=stat_sems.at[0],
+        recv_sem=stat_sems.at[1],
+        device_id={"chan": 1 - core},
+        device_id_type=MESH,
+    )
+    stats.start()
+    stats.wait()
+    inverse_rms = lax.rsqrt((stat_send[0] + stat_recv[0]) / channel_total + epsilon_value)
+    cross_mean = (stat_send[1] + stat_recv[1]) / channel_total
+    cubed = inverse_rms * inverse_rms * inverse_rms * cross_mean
+
+    def differentiate(tile, carry):
+        at = lanes(tile)
+        queries = q_ref[:, at].astype(f32)
+        activated = queries * mixed_ref[tile]
+        scaled = g_ref[:, at].astype(f32) * norm_ref[:, at]
+        mix_grad = (inverse_rms * scaled - activated * cubed) * queries
+        mix_ref[tile] = mix_grad
+        pack(MIXGRAD, tile, mix_grad)
+        return carry
+
+    lax.fori_loop(0, pairs, differentiate, 0)
+    send_all(MIXGRAD)
+
+    def first_outputs(tile, carry):
+        at = lanes(tile)
+        mixed = mixed_ref[tile]
+        activated = q_ref[:, at].astype(f32) * mixed
+        scaled = g_ref[:, at].astype(f32) * norm_ref[:, at]
+        out_ref[:, at] = (activated * inverse_rms * norm_ref[:, at]).astype(out_ref.dtype)
+        qg_ref[:, at] = ((inverse_rms * scaled - activated * cubed) * mixed).astype(qg_ref.dtype)
+        return carry
+
+    lax.fori_loop(0, pairs, first_outputs, 0)
+    receive_all(MIXGRAD)
+    spectrum(MIXGRAD, m_spec, m_swap)
+    correlate(h_spec, h_swap)
+    invert(INPUT, False)
+    send_all(INPUT)
+    correlate(x_spec, x_swap)
+    invert(FGRAD, False)
+    send_all(FGRAD)
+    receive_all(INPUT)
+
+    def input_outputs(tile, carry):
+        at = lanes(tile)
+        gated_grad = unpack(INPUT, tile) + skip_ref[:, at] * mix_ref[tile]
+        kg_ref[:, at] = (gated_grad * v_ref[:, at].astype(f32)).astype(kg_ref.dtype)
+        vg_ref[:, at] = (gated_grad * k_ref[:, at].astype(f32)).astype(vg_ref.dtype)
+        return carry
+
+    lax.fori_loop(0, pairs, input_outputs, 0)
+    receive_all(FGRAD)
+
+    def filter_outputs(tile, carry):
+        fg_ref[:, lanes(tile)] = unpack(FGRAD, tile)
+        return carry
+
+    lax.fori_loop(0, pairs, filter_outputs, 0)
+    for unit in range(6):
+        sent_all(unit)
+
+
+def fast_body(query_proj, key_proj, value_proj, long_filter, skip_gain, norm_gain, out_grad):
+    rows, width = query_proj.shape
+    seq_count = lax.axis_size("seq")
+    pairs = seq_count // 2
+    forward, inverse = block_matrices(rows)
+    vmem = pl.BlockSpec(memory_space=pltpu.VMEM)
+    spec = pltpu.VMEM((pairs, 2 * rows, 128), jnp.float32)
+    blocks = pltpu.VMEM((6, seq_count, rows // 2, 128), jnp.float32)
+    held = pltpu.VMEM((pairs, rows, 128), jnp.float32)
+    stat = pltpu.VMEM((2, rows, 128), jnp.float32)
+    narrow = jax.ShapeDtypeStruct((rows, width), jnp.bfloat16)
+    return pl.pallas_call(
+        functools.partial(fast_kernel, seq_count),
+        out_shape=(narrow,) * 4 + (jax.ShapeDtypeStruct((rows, width), jnp.float32),),
+        in_specs=[vmem] * 9,
+        out_specs=(vmem,) * 5,
+        scratch_shapes=[
+            blocks, blocks, spec, spec, spec, spec, spec, spec, spec,
+            pltpu.VMEM((pairs + 2, 2 * rows, 128), jnp.float32),
+            held, held, stat, stat,
+            pltpu.SemaphoreType.DMA((6, seq_count)),
+            pltpu.SemaphoreType.DMA((6, seq_count)),
+            pltpu.SemaphoreType.DMA((2,)),
+        ],
+        compiler_params=pltpu.CompilerParams(
+            collective_id=0, has_side_effects=True, vmem_limit_bytes=40 * 1024 * 1024
+        ),
+        cost_estimate=pl.CostEstimate(
+            flops=2 * 10**9, bytes_accessed=4 * 10**6, transcendentals=rows * 128
+        ),
+    )(
+        query_proj, key_proj, value_proj, long_filter,
+        skip_gain[None, :], norm_gain[None, :], out_grad, forward, inverse,
+    )
+
+
+def choose_body(mesh, *arrays):
+    rows, width = arrays[0].shape
+    seq_count = mesh.shape["seq"]
+    fits = width == 64 * seq_count and rows == 128 and seq_count % 4 == 0
+    if fits and mesh.shape["chan"] == 2:
+        return fast_body(*arrays)
+    return wide_body(*arrays)
+
+
 def solution(mesh):
     return jax.shard_map(
-        body,
+        functools.partial(choose_body, mesh),
         mesh=mesh,
         in_specs=(
             P("seq", "chan"),

time: 488 us -> 107 us (0.22)
  the two profiles are of different devices: /device:TPU:0 before, /device:TPU:8 now
where the time goes in v1:
time: 107 us
  Pallas kernels  94.1 us (88%)
  local copies, waits for them, and re-layouts  11.7 us (11%)
    pallas_call x1, Pallas kernels, fast_body(): pl.pallas_call(functools.partial(fast_kernel, seq_count), out_shape=(narr...  94.1 us
    unnamed x23, local copies, waits for them, and re-layouts  11.7 us

profile of v1, /device:TPU:8, one launch (start us, length us, event | category | flops | bytes accessed | tf_op | source)
XLA Modules:
  0.0 106.5 jit_solution(12614865248174987739)
XLA Ops:
  0.6 0.0 copy-start
  0.6 1.0 copy-done
  1.7 0.0 copy-start.1
  1.7 0.9 copy-done.1
  2.6 0.0 copy-start.2
  2.6 0.9 copy-done.2
  3.6 0.0 copy-start.3
  3.6 0.9 copy-done.3
  4.5 0.0 copy-start.4
  4.5 0.9 copy-done.4
  5.5 0.0 copy-start.5
  5.5 0.7 copy-done.5
  6.2 0.0 copy-start.6
  6.2 0.7 copy-done.6
  6.9 0.0 copy-start.7
  6.9 1.0 copy-done.7
  7.8 0.0 copy-start.8
  7.9 0.9 copy-done.8
  8.8 94.1 %shard_map.128 = (bf16[128,1024]{1,0:T(8,128)(2,1)S(1)}, bf16[128,1024]{1,0:T(8,128)(2,1)S(1)}, bf16[128,1024]{1,0:T(8,128)(2,1)S(1)}, bf16[128,1024]{1,0:T(8,128)(2,1)S(1)}, f32[128,1024]{1,0:T(8,128)S(1)}) custom-call(bf16[128,1024]{1,0:T(8,128)(2,1)S(1)} %copy-done.1, bf16[128,1024]{1,0:T(8,128)(2,1)S(1)} %copy-done.2, bf16[128,1024]{1,0:T(8,128)(2,1)S(1)} %copy-done.3, ...), custom_call_target="tpu_custom_call" | custom-call | flops 2000000000 | bytes 4000000 | tf_op jit(solution)/shard_map/pallas_call | solution.py:478
  102.9 0.7 copy.19
  103.6 0.7 copy.20
  104.3 0.7 copy.21
  105.0 0.7 copy.22
  105.7 0.8 copy.23
Async XLA Ops:
  0.6 1.0 copy-start
  1.7 0.9 copy-start.1
  2.6 0.9 copy-start.2
  3.6 0.9 copy-start.3
  4.5 0.9 copy-start.4
  5.5 0.7 copy-start.5
  6.2 0.7 copy-start.6
  6.9 1.0 copy-start.7
  7.8 0.9 copy-start.8

commit v2 on v1

--- a/solution.py
+++ b/solution.py
@@ -171,11 +171,14 @@
 
 def fast_kernel(
     seq_count,
+    q_hbm, k_hbm, v_hbm, f_hbm, skip_hbm, norm_hbm, g_hbm, fwd_hbm, inv_hbm,
+    out_hbm, qg_hbm, kg_hbm, vg_hbm, fg_hbm,
+    out_ref, qg_ref, kg_ref, vg_ref, fg_ref,
     q_ref, k_ref, v_ref, f_ref, skip_ref, norm_ref, g_ref, fwd_ref, inv_ref,
-    out_ref, qg_ref, kg_ref, vg_ref, fg_ref,
     send, recv, h_spec, h_swap, x_spec, x_swap, m_spec, m_swap, z_spec, fields,
+    even_ref, odd_ref, back_ref,
     mixed_ref, mix_ref, stat_send, stat_recv,
-    send_sems, recv_sems, stat_sems,
+    send_sems, recv_sems, stat_sems, load_sems, store_sems,
 ):
     rows, width = q_ref.shape
     half = rows // 2
@@ -184,6 +187,24 @@
     me = lax.axis_index("seq")
     core = lax.axis_index("chan")
     f32 = jnp.float32
+
+    loads = [
+        pltpu.make_async_copy(source, target, load_sems.at[place])
+        for place, (source, target) in enumerate([
+            (f_hbm, f_ref), (k_hbm, k_ref), (v_hbm, v_ref), (fwd_hbm, fwd_ref),
+            (inv_hbm, inv_ref), (q_hbm, q_ref), (g_hbm, g_ref), (skip_hbm, skip_ref),
+            (norm_hbm, norm_ref),
+        ])
+    ]
+    for copy in loads:
+        copy.start()
+    stores = [
+        pltpu.make_async_copy(source, target, store_sems.at[place])
+        for place, (source, target) in enumerate([
+            (out_ref, out_hbm), (qg_ref, qg_hbm), (kg_ref, kg_hbm), (vg_ref, vg_hbm),
+            (fg_ref, fg_hbm),
+        ])
+    ]
 
     barrier = pltpu.get_barrier_semaphore()
 
@@ -227,82 +248,114 @@
             device_id_type=MESH,
         )
 
+    my_pair, my_side = me // 2, lax.rem(me, 2)
+
+    def pair_at(step):
+        odd_step = lax.rem(step, 2)
+        flips = odd_step * ((step + 1) // 2) + (1 - odd_step) * (pairs // 2 + step // 2)
+        pair, bit = 0, 1
+        while bit < pairs:
+            mine, flip = lax.rem(my_pair // bit, 2), lax.rem(flips // bit, 2)
+            pair = pair + bit * (mine + flip - 2 * mine * flip)
+            bit *= 2
+        return pair
+
+    def peers_at(step):
+        return 2 * pair_at(step) + my_side, 2 * pair_at(step) + 1 - my_side
+
+    neighbour = 2 * my_pair + 1 - my_side
+
     def send_all(unit):
+        remote(unit, neighbour, me, neighbour, neighbour, me).start()
+
         def one(step, carry):
-            peer = lax.rem(me + step, seq_count)
-            remote(unit, peer, me, peer, peer, me).start()
-            return carry
-
-        lax.fori_loop(1, seq_count, one, 0)
+            for peer in peers_at(step):
+                remote(unit, peer, me, peer, peer, me).start()
+            return carry
+
+        lax.fori_loop(0, pairs - 1, one, 0)
         recv[unit, me] = send[unit, me]
 
-    def receive_all(unit):
+    def receive_each(unit, use, carry):
+        remote(unit, neighbour, neighbour, neighbour, neighbour, neighbour).wait_recv()
+        carry = use(my_pair, carry)
+
         def one(step, carry):
-            peer = lax.rem(me + seq_count - step, seq_count)
-            remote(unit, peer, peer, peer, peer, peer).wait_recv()
-            return carry
-
-        lax.fori_loop(1, seq_count, one, 0)
+            for peer in peers_at(step):
+                remote(unit, peer, peer, peer, peer, peer).wait_recv()
+            return use(pair_at(step), carry)
+
+        return lax.fori_loop(0, pairs - 1, one, carry)
 
     def sent_all(unit):
+        remote(unit, neighbour, me, neighbour, neighbour, me).wait_send()
+
         def one(step, carry):
-            peer = lax.rem(me + step, seq_count)
-            remote(unit, peer, me, peer, peer, me).wait_send()
-            return carry
-
-        lax.fori_loop(1, seq_count, one, 0)
-
-    def spectrum(unit, spec, swapped):
-        def one(step, carry):
-            block = jnp.concatenate([unpack(unit, 2 * step), unpack(unit, 2 * step + 1)], 1)
-            field = split_dot(fwd_ref[...], block)
-            for side in range(2):
-                part = field[:, 128 * side:128 * side + 128]
-                spec[2 * step + side] = part
-                swapped[2 * step + side] = swap(part)
-            return carry
-
-        lax.fori_loop(0, pairs // 2, one, 0)
+            for peer in peers_at(step):
+                remote(unit, peer, me, peer, peer, me).wait_send()
+            return carry
+
+        lax.fori_loop(0, pairs - 1, one, 0)
+
+    def transform(unit, spec, swapped, pair):
+        field = split_dot(fwd_ref[...], unpack(unit, pair))
+        spec[pair] = field
+        swapped[pair] = swap(field)
+
+    def clear_sums():
+        def one(pair, carry):
+            z_spec[pair] = jnp.zeros((2 * rows, 128), f32)
+            return carry
+
+        lax.fori_loop(0, pairs, one, 0)
+
+    def lay_out_filter():
+        def one(pair, carry):
+            left = first_lanes(2 * rows)
+            nothing = jnp.zeros((2 * rows, 128), f32)
+            even_ref[pair] = nothing
+            odd_ref[pair] = nothing
+            back_ref[pair] = nothing
+            here, there = h_spec[pair], h_swap[pair]
+            before = lax.rem(pair + pairs - 1, pairs)
+            started = jnp.where(pair > 0, 1.0, 0.0)
+            even_ref[pairs + pair] = jnp.where(left, here, there)
+            odd_ref[pairs + pair] = jnp.where(left, h_swap[before] * started, here)
+            back_ref[pairs + pair] = jnp.where(left, there, h_spec[before] * started)
+            return carry
+
+        lax.fori_loop(0, pairs, one, 0)
+
+    def add_products(spec, swapped, pair, forward):
+        def one(tile, carry):
+            first = pl.multiple_of(tile * 8, 8)
+            real_rows, imag_rows = pl.ds(first, 8), pl.ds(first + rows, 8)
+            xr, xi = spec[pair, real_rows, :], spec[pair, imag_rows, :]
+            yr, yi = swapped[pair, real_rows, :], swapped[pair, imag_rows, :]
+            for n in range(pairs):
+                if forward:
+                    place, cross = pairs + n - pair, odd_ref
+                else:
+                    place, cross = pairs + pair - n, back_ref
+                er, ei = even_ref[place, real_rows, :], even_ref[place, imag_rows, :]
+                tr, ti = cross[place, real_rows, :], cross[place, imag_rows, :]
+                if forward:
+                    real = (xr * er - xi * ei) + (yr * tr - yi * ti)
+                    imag = (xr * ei + xi * er) + (yr * ti + yi * tr)
+                else:
+                    real = (xr * er + xi * ei) + (yr * tr + yi * ti)
+                    imag = (xi * er - xr * ei) + (yi * tr - yr * ti)
+                z_spec[n, real_rows, :] = z_spec[n, real_rows, :] + real
+                z_spec[n, imag_rows, :] = z_spec[n, imag_rows, :] + imag
+            return carry
+
+        lax.fori_loop(0, rows // 8, one, 0)
 
     def load(ref, tile, count):
         first = pl.multiple_of(tile * 8, 8)
         real = [ref[k, pl.ds(first, 8), :] for k in range(count)]
         imag = [ref[k, pl.ds(first + rows, 8), :] for k in range(count)]
         return real, imag
-
-    def convolve():
-        def one(tile, carry):
-            left = first_lanes(8)
-            zero = jnp.zeros((8, 128), f32)
-            hr, hi = load(h_spec, tile, pairs)
-            sr, si = load(h_swap, tile, pairs)
-            xr, xi = load(x_spec, tile, pairs)
-            yr, yi = load(x_swap, tile, pairs)
-            even = [
-                (jnp.where(left, hr[k], sr[k]), jnp.where(left, hi[k], si[k]))
-                for k in range(pairs)
-            ]
-            odd = [
-                (
-                    jnp.where(left, sr[k - 1] if k else zero, hr[k]),
-                    jnp.where(left, si[k - 1] if k else zero, hi[k]),
-                )
-                for k in range(pairs)
-            ]
-            first = pl.multiple_of(tile * 8, 8)
-            for n in range(pairs):
-                real, imag = zero, zero
-                for k in range(n + 1):
-                    er, ei = even[k]
-                    tr, ti = odd[k]
-                    m = n - k
-                    real = real + (xr[m] * er - xi[m] * ei) + (yr[m] * tr - yi[m] * ti)
-                    imag = imag + (xr[m] * ei + xi[m] * er) + (yr[m] * ti + yi[m] * tr)
-                z_spec[n, pl.ds(first, 8), :] = real
-                z_spec[n, pl.ds(first + rows, 8), :] = imag
-            return carry
-
-        lax.fori_loop(0, rows // 8, one, 0)
 
     def correlate(spec, swapped):
         def one(tile, carry):
@@ -368,6 +421,8 @@
         pack(GATED, tile, k_ref[:, at].astype(f32) * v_ref[:, at].astype(f32))
         return carry
 
+    for copy in loads[:3]:
+        copy.wait()
     lax.fori_loop(0, pairs, pack_inputs, 0)
     fields[0] = jnp.zeros((2 * rows, 128), f32)
     fields[pairs + 1] = jnp.zeros((2 * rows, 128), f32)
@@ -375,14 +430,26 @@
     pl.semaphore_wait(barrier, seq_count)
     send_all(FILTER)
     send_all(GATED)
-    receive_all(FILTER)
-    spectrum(FILTER, h_spec, h_swap)
-    receive_all(GATED)
-    spectrum(GATED, x_spec, x_swap)
-    convolve()
+    for copy in loads[3:]:
+        copy.wait()
+    clear_sums()
+
+    def take_filter(pair, carry):
+        transform(FILTER, h_spec, h_swap, pair)
+        return carry
+
+    receive_each(FILTER, take_filter, 0)
+    lay_out_filter()
+
+    def take_gated(pair, carry):
+        transform(GATED, x_spec, x_swap, pair)
+        add_products(x_spec, x_swap, pair, True)
+        return carry
+
+    receive_each(GATED, take_gated, 0)
     invert(CONV, True)
     send_all(CONV)
-    receive_all(CONV)
+    clear_sums()
 
     def activate(tile, carry):
         squares, crosses = carry
@@ -395,7 +462,7 @@
         return squares + activated * activated, crosses + scaled * activated
 
     nothing = jnp.zeros((rows, 128), f32)
-    squares, crosses = lax.fori_loop(0, pairs, activate, (nothing, nothing))
+    squares, crosses = receive_each(CONV, activate, (nothing, nothing))
     stat_send[0] = jnp.broadcast_to(jnp.sum(squares, axis=1, keepdims=True), (rows, 128))
     stat_send[1] = jnp.broadcast_to(jnp.sum(crosses, axis=1, keepdims=True), (rows, 128))
     stats = pltpu.make_async_remote_copy(
@@ -435,16 +502,20 @@
         return carry
 
     lax.fori_loop(0, pairs, first_outputs, 0)
-    receive_all(MIXGRAD)
-    spectrum(MIXGRAD, m_spec, m_swap)
-    correlate(h_spec, h_swap)
+    for copy in stores[:2]:
+        copy.start()
+
+    def take_grad(pair, carry):
+        transform(MIXGRAD, m_spec, m_swap, pair)
+        add_products(m_spec, m_swap, pair, False)
+        return carry
+
+    receive_each(MIXGRAD, take_grad, 0)
     invert(INPUT, False)
     send_all(INPUT)
     correlate(x_spec, x_swap)
     invert(FGRAD, False)
     send_all(FGRAD)
-    receive_all(INPUT)
-
     def input_outputs(tile, carry):
         at = lanes(tile)
         gated_grad = unpack(INPUT, tile) + skip_ref[:, at] * mix_ref[tile]
@@ -452,16 +523,32 @@
         vg_ref[:, at] = (gated_grad * k_ref[:, at].astype(f32)).astype(vg_ref.dtype)
         return carry
 
-    lax.fori_loop(0, pairs, input_outputs, 0)
-    receive_all(FGRAD)
+    receive_each(INPUT, input_outputs, 0)
+    for copy in stores[2:4]:
+        copy.start()
 
     def filter_outputs(tile, carry):
         fg_ref[:, lanes(tile)] = unpack(FGRAD, tile)
         return carry
 
-    lax.fori_loop(0, pairs, filter_outputs, 0)
+    receive_each(FGRAD, filter_outputs, 0)
+    stores[4].start()
     for unit in range(6):
         sent_all(unit)
+    for copy in stores:
+        copy.wait()
+
+
+def write_kernel(count, *refs):
+    held, written, sems = refs[:count], refs[count:2 * count], refs[2 * count]
+    copies = [
+        pltpu.make_async_copy(source, target, sems.at[place])
+        for place, (source, target) in enumerate(zip(held, written))
+    ]
+    for copy in copies:
+        copy.start()
+    for copy in copies:
+        copy.wait()
 
 
 def fast_body(query_proj, key_proj, value_proj, long_filter, skip_gain, norm_gain, out_grad):
@@ -469,41 +556,56 @@
     seq_count = lax.axis_size("seq")
     pairs = seq_count // 2
     forward, inverse = block_matrices(rows)
-    vmem = pl.BlockSpec(memory_space=pltpu.VMEM)
+    operands = (
+        query_proj, key_proj, value_proj, long_filter,
+        skip_gain[None, :], norm_gain[None, :], out_grad, forward, inverse,
+    )
+    anywhere = pl.BlockSpec(memory_space=pltpu.HBM)
     spec = pltpu.VMEM((pairs, 2 * rows, 128), jnp.float32)
+    laid = pltpu.VMEM((2 * pairs, 2 * rows, 128), jnp.float32)
     blocks = pltpu.VMEM((6, seq_count, rows // 2, 128), jnp.float32)
     held = pltpu.VMEM((pairs, rows, 128), jnp.float32)
     stat = pltpu.VMEM((2, rows, 128), jnp.float32)
     narrow = jax.ShapeDtypeStruct((rows, width), jnp.bfloat16)
-    return pl.pallas_call(
+    shapes = (narrow,) * 4 + (jax.ShapeDtypeStruct((rows, width), jnp.float32),)
+    results = pl.pallas_call(
         functools.partial(fast_kernel, seq_count),
-        out_shape=(narrow,) * 4 + (jax.ShapeDtypeStruct((rows, width), jnp.float32),),
-        in_specs=[vmem] * 9,
-        out_specs=(vmem,) * 5,
-        scratch_shapes=[
+        out_shape=shapes,
+        in_specs=[anywhere] * len(operands),
+        out_specs=(anywhere,) * 5,
+        scratch_shapes=[pltpu.VMEM(one.shape, one.dtype) for one in shapes + operands] + [
             blocks, blocks, spec, spec, spec, spec, spec, spec, spec,
             pltpu.VMEM((pairs + 2, 2 * rows, 128), jnp.float32),
+            laid, laid, laid,
             held, held, stat, stat,
             pltpu.SemaphoreType.DMA((6, seq_count)),
             pltpu.SemaphoreType.DMA((6, seq_count)),
             pltpu.SemaphoreType.DMA((2,)),
+            pltpu.SemaphoreType.DMA((len(operands),)),
+            pltpu.SemaphoreType.DMA((len(shapes),)),
         ],
         compiler_params=pltpu.CompilerParams(
-            collective_id=0, has_side_effects=True, vmem_limit_bytes=40 * 1024 * 1024
+            collective_id=0, has_side_effects=True, vmem_limit_bytes=62 * 1024 * 1024
         ),
         cost_estimate=pl.CostEstimate(
             flops=2 * 10**9, bytes_accessed=4 * 10**6, transcendentals=rows * 128
         ),
-    )(
-        query_proj, key_proj, value_proj, long_filter,
-        skip_gain[None, :], norm_gain[None, :], out_grad, forward, inverse,
-    )
+    )(*operands)
+    return pl.pallas_call(
+        functools.partial(write_kernel, len(shapes)),
+        out_shape=shapes,
+        in_specs=[anywhere] * len(shapes),
+        out_specs=(anywhere,) * len(shapes),
+        scratch_shapes=[pltpu.SemaphoreType.DMA((len(shapes),))],
+        compiler_params=pltpu.CompilerParams(vmem_limit_bytes=62 * 1024 * 1024),
+    )(*results)
 
 
 def choose_body(mesh, *arrays):
     rows, width = arrays[0].shape
     seq_count = mesh.shape["seq"]
-    fits = width == 64 * seq_count and rows == 128 and seq_count % 4 == 0
+    power = seq_count & (seq_count - 1) == 0
+    fits = width == 64 * seq_count and rows == 128 and seq_count >= 4 and power
     if fits and mesh.shape["chan"] == 2:
         return fast_body(*arrays)
     return wide_body(*arrays)

time: 107 us -> 144 us (1.35)
  Pallas kernels: 94.1 us -> 143 us
  local copies, waits for them, and re-layouts: 11.7 us -> 0 us
    pallas_call x1 -> x2, Pallas kernels: 94.1 us -> 143 us  [the longest x1 94.2 us: fast_body(): pl.pallas_call(functools.partial(fast_kernel, seq_count), out_shape=shape...]
    unnamed x23 -> x0, local copies, waits for them, and re-layouts: 11.7 us -> none
where the time goes in v2:
time: 144 us
  Pallas kernels  143 us (99%)
    pallas_call x1, Pallas kernels, fast_body(): pl.pallas_call(functools.partial(fast_kernel, seq_count), out_shape=shape...  94.2 us
    pallas_call x1, Pallas kernels, fast_body(): pl.pallas_call(functools.partial(write_kernel, len(shapes)), out_shape=sh...  48.8 us

profile of v2, /device:TPU:8, one launch (start us, length us, event | category | flops | bytes accessed | tf_op | source)
XLA Modules:
  0.0 143.6 jit_solution(15116333576913417009)
XLA Ops:
  0.6 94.2 %shard_map.128 = (bf16[128,1024]{1,0:T(8,128)(2,1)}, bf16[128,1024]{1,0:T(8,128)(2,1)}, bf16[128,1024]{1,0:T(8,128)(2,1)}, bf16[128,1024]{1,0:T(8,128)(2,1)}, f32[128,1024]{1,0:T(8,128)}) custom-call(bf16[128,1024]{1,0:T(8,128)(2,1)} %q_hbm.1, bf16[128,1024]{1,0:T(8,128)(2,1)} %k_hbm.1, bf16[128,1024]{1,0:T(8,128)(2,1)} %v_hbm.1, f32[128,1024]{1,0:T(8,128)} %f_hbm.1, ...), custom_call_target="tpu_custom_call" | custom-call | flops 2000000000 | bytes 4000000 | tf_op jit(solution)/shard_map/pallas_call | solution.py:571
  94.8 48.8 %shard_map.129 = (bf16[128,1024]{1,0:T(8,128)(2,1)}, bf16[128,1024]{1,0:T(8,128)(2,1)}, bf16[128,1024]{1,0:T(8,128)(2,1)}, bf16[128,1024]{1,0:T(8,128)(2,1)}, f32[128,1024]{1,0:T(8,128)}) custom-call(bf16[128,1024]{1,0:T(8,128)(2,1)} %get-tuple-element.10.refs_0_, bf16[128,1024]{1,0:T(8,128)(2,1)} %get-tuple-element.11.refs_1_, ...), custom_call_target="tpu_custom_call" | custom-call | tf_op jit(solution)/shard_map/pallas_call | solution.py:594

commit v3 on v2

--- a/solution.py
+++ b/solution.py
@@ -250,9 +250,7 @@
 
     my_pair, my_side = me // 2, lax.rem(me, 2)
 
-    def pair_at(step):
-        odd_step = lax.rem(step, 2)
-        flips = odd_step * ((step + 1) // 2) + (1 - odd_step) * (pairs // 2 + step // 2)
+    def pair_at(flips):
         pair, bit = 0, 1
         while bit < pairs:
             mine, flip = lax.rem(my_pair // bit, 2), lax.rem(flips // bit, 2)
@@ -260,42 +258,58 @@
             bit *= 2
         return pair
 
-    def peers_at(step):
-        return 2 * pair_at(step) + my_side, 2 * pair_at(step) + 1 - my_side
-
-    neighbour = 2 * my_pair + 1 - my_side
+    odd_plane = lax.rem(my_pair // 2, 2)
+
+    def send_flips(step):
+        later, turn = step // 4, lax.rem(step, 4)
+        plane = odd_plane + later - 2 * odd_plane * later
+        return 4 * (1 - lax.rem(turn, 2)) + 2 * plane + turn // 2
+
+    def receive_flips(step):
+        turn = step // 2
+        return 4 * (1 - lax.rem(turn, 2)) + 2 * lax.rem(step, 2) + turn // 2
+
+    def for_peers(flips, use):
+        pair = pair_at(flips)
+        use(2 * pair + 1 - my_side)
+
+        @pl.when(flips > 0)
+        def _():
+            use(2 * pair + my_side)
+
+        return pair
 
     def send_all(unit):
-        remote(unit, neighbour, me, neighbour, neighbour, me).start()
+        recv[unit, me] = send[unit, me]
 
         def one(step, carry):
-            for peer in peers_at(step):
-                remote(unit, peer, me, peer, peer, me).start()
-            return carry
-
-        lax.fori_loop(0, pairs - 1, one, 0)
-        recv[unit, me] = send[unit, me]
+            for_peers(
+                send_flips(step),
+                lambda peer: remote(unit, peer, me, peer, peer, me).start(),
+            )
+            return carry
+
+        lax.fori_loop(0, pairs, one, 0)
 
     def receive_each(unit, use, carry):
-        remote(unit, neighbour, neighbour, neighbour, neighbour, neighbour).wait_recv()
-        carry = use(my_pair, carry)
-
         def one(step, carry):
-            for peer in peers_at(step):
-                remote(unit, peer, peer, peer, peer, peer).wait_recv()
-            return use(pair_at(step), carry)
-
-        return lax.fori_loop(0, pairs - 1, one, carry)
+            pair = for_peers(
+                receive_flips(step),
+                lambda peer: remote(unit, peer, peer, peer, peer, peer).wait_recv(),
+            )
+            return use(pair, carry)
+
+        return lax.fori_loop(0, pairs, one, carry)
 
     def sent_all(unit):
-        remote(unit, neighbour, me, neighbour, neighbour, me).wait_send()
-
         def one(step, carry):
-            for peer in peers_at(step):
-                remote(unit, peer, me, peer, peer, me).wait_send()
-            return carry
-
-        lax.fori_loop(0, pairs - 1, one, 0)
+            for_peers(
+                send_flips(step),
+                lambda peer: remote(unit, peer, me, peer, peer, me).wait_send(),
+            )
+            return carry
+
+        lax.fori_loop(0, pairs, one, 0)
 
     def transform(unit, spec, swapped, pair):
         field = split_dot(fwd_ref[...], unpack(unit, pair))
@@ -540,14 +554,22 @@
 
 
 def write_kernel(count, *refs):
-    held, written, sems = refs[:count], refs[count:2 * count], refs[2 * count]
-    copies = [
-        pltpu.make_async_copy(source, target, sems.at[place])
-        for place, (source, target) in enumerate(zip(held, written))
+    read, written, held = (refs[count * part:count * part + count] for part in range(3))
+    sems = refs[3 * count]
+    inward = [
+        pltpu.make_async_copy(read[place], held[place], sems.at[0, place])
+        for place in range(count)
     ]
-    for copy in copies:
+    outward = [
+        pltpu.make_async_copy(held[place], written[place], sems.at[1, place])
+        for place in range(count)
+    ]
+    for copy in inward:
         copy.start()
-    for copy in copies:
+    for first, second in zip(inward, outward):
+        first.wait()
+        second.start()
+    for copy in outward:
         copy.wait()
 
 
@@ -596,7 +618,8 @@
         out_shape=shapes,
         in_specs=[anywhere] * len(shapes),
         out_specs=(anywhere,) * len(shapes),
-        scratch_shapes=[pltpu.SemaphoreType.DMA((len(shapes),))],
+        scratch_shapes=[pltpu.VMEM(one.shape, one.dtype) for one in shapes]
+        + [pltpu.SemaphoreType.DMA((2, len(shapes)))],
         compiler_params=pltpu.CompilerParams(vmem_limit_bytes=62 * 1024 * 1024),
     )(*results)
 
@@ -604,8 +627,7 @@
 def choose_body(mesh, *arrays):
     rows, width = arrays[0].shape
     seq_count = mesh.shape["seq"]
-    power = seq_count & (seq_count - 1) == 0
-    fits = width == 64 * seq_count and rows == 128 and seq_count >= 4 and power
+    fits = width == 64 * seq_count and rows == 128 and seq_count == 16
     if fits and mesh.shape["chan"] == 2:
         return fast_body(*arrays)
     return wide_body(*arrays)

time: 144 us -> 97.8 us (0.68)
  Pallas kernels: 143 us -> 97 us
    pallas_call x1, Pallas kernels: 48.8 us -> 2.24 us  [fast_body(): pl.pallas_call(functools.partial(write_kernel, len(shapes)), out_shape=sh...]
where the time goes in v3:
time: 97.8 us; the launch traced here: 97.6 us
  Pallas kernels  97 us (99%)
    pallas_call x1, Pallas kernels, fast_body(): pl.pallas_call(functools.partial(fast_kernel, seq_count), out_shape=shape...  94.7 us
    pallas_call x1, Pallas kernels, fast_body(): pl.pallas_call(functools.partial(write_kernel, len(shapes)), out_shape=sh...  2.24 us

profile of v3, /device:TPU:8, one launch (start us, length us, event | category | flops | bytes accessed | tf_op | source)
XLA Modules:
  0.0 97.6 jit_solution(16170807997234368146)
XLA Ops:
  0.6 94.7 %shard_map.128 = (bf16[128,1024]{1,0:T(8,128)(2,1)}, bf16[128,1024]{1,0:T(8,128)(2,1)}, bf16[128,1024]{1,0:T(8,128)(2,1)}, bf16[128,1024]{1,0:T(8,128)(2,1)}, f32[128,1024]{1,0:T(8,128)}) custom-call(bf16[128,1024]{1,0:T(8,128)(2,1)} %q_hbm.1, bf16[128,1024]{1,0:T(8,128)(2,1)} %k_hbm.1, bf16[128,1024]{1,0:T(8,128)(2,1)} %v_hbm.1, f32[128,1024]{1,0:T(8,128)} %f_hbm.1, ...), custom_call_target="tpu_custom_call" | custom-call | flops 2000000000 | bytes 4000000 | tf_op jit(solution)/shard_map/pallas_call | solution.py:593
  95.4 2.2 %shard_map.129 = (bf16[128,1024]{1,0:T(8,128)(2,1)}, bf16[128,1024]{1,0:T(8,128)(2,1)}, bf16[128,1024]{1,0:T(8,128)(2,1)}, bf16[128,1024]{1,0:T(8,128)(2,1)}, f32[128,1024]{1,0:T(8,128)}) custom-call(bf16[128,1024]{1,0:T(8,128)(2,1)} %get-tuple-element.10.refs_0_, bf16[128,1024]{1,0:T(8,128)(2,1)} %get-tuple-element.11.refs_1_, ...), custom_call_target="tpu_custom_call" | custom-call | tf_op jit(solution)/shard_map/pallas_call | solution.py:616

commit v4 on v3

--- a/solution.py
+++ b/solution.py
@@ -157,7 +157,7 @@
     places = np.arange(2 * rows)
     angles = np.pi / (2 * rows) * (freqs[:, None] * places[None, :] % (4 * rows))
     forward = np.concatenate([np.cos(angles), -np.sin(angles)], 0)[:, :rows]
-    inverse = np.concatenate([np.cos(angles), -np.sin(angles)], 0).T / rows
+    inverse = np.concatenate([np.cos(angles), -np.sin(angles)], 0)[:, :rows].T / rows
     return split_matrix(forward), split_matrix(inverse)
 
 
@@ -175,7 +175,7 @@
     out_hbm, qg_hbm, kg_hbm, vg_hbm, fg_hbm,
     out_ref, qg_ref, kg_ref, vg_ref, fg_ref,
     q_ref, k_ref, v_ref, f_ref, skip_ref, norm_ref, g_ref, fwd_ref, inv_ref,
-    send, recv, h_spec, h_swap, x_spec, x_swap, m_spec, m_swap, z_spec, fields,
+    send, recv, h_spec, h_swap, x_spec, x_swap, m_spec, m_swap, z_spec,
     even_ref, odd_ref, back_ref,
     mixed_ref, mix_ref, stat_send, stat_recv,
     send_sems, recv_sems, stat_sems, load_sems, store_sems,
@@ -279,14 +279,18 @@
 
         return pair
 
-    def send_all(unit):
-        recv[unit, me] = send[unit, me]
-
+    def send_tiles(unit, make):
         def one(step, carry):
-            for_peers(
-                send_flips(step),
-                lambda peer: remote(unit, peer, me, peer, peer, me).start(),
-            )
+            flips = send_flips(step)
+            if make is not None:
+                pair = pair_at(flips)
+                pack(unit, pair, make(pair))
+            for_peers(flips, lambda peer: remote(unit, peer, me, peer, peer, me).start())
+
+            @pl.when(flips == 0)
+            def _():
+                recv[unit, me] = send[unit, me]
+
             return carry
 
         lax.fori_loop(0, pairs, one, 0)
@@ -323,19 +327,39 @@
 
         lax.fori_loop(0, pairs, one, 0)
 
-    def lay_out_filter():
+    def add_before(spec, swapped, new_spec, new_swapped):
+        def one(pair, carry):
+            left = first_lanes(rows)
+            odd_row = lax.rem(lax.broadcasted_iota(jnp.int32, (rows, 128), 0), 2) == 1
+            before = lax.rem(pair + pairs - 1, pairs)
+            started = jnp.where(pair > 0, 1.0, 0.0)
+            real = jnp.where(left, swapped[before, :rows, :] * started, swapped[pair, :rows, :])
+            imag = jnp.where(left, swapped[before, rows:, :] * started, swapped[pair, rows:, :])
+            turned_real = jnp.where(odd_row, imag, -imag)
+            turned_imag = jnp.where(odd_row, -real, real)
+            real = spec[pair, :rows, :] + turned_real
+            imag = spec[pair, rows:, :] + turned_imag
+            new_spec[pair, :rows, :] = real
+            new_spec[pair, rows:, :] = imag
+            new_swapped[pair, :rows, :] = swap(real)
+            new_swapped[pair, rows:, :] = swap(imag)
+            return carry
+
+        lax.fori_loop(0, pairs, one, 0)
+
+    def lay_out(spec, swapped):
         def one(pair, carry):
             left = first_lanes(2 * rows)
             nothing = jnp.zeros((2 * rows, 128), f32)
             even_ref[pair] = nothing
             odd_ref[pair] = nothing
             back_ref[pair] = nothing
-            here, there = h_spec[pair], h_swap[pair]
+            here, there = spec[pair], swapped[pair]
             before = lax.rem(pair + pairs - 1, pairs)
             started = jnp.where(pair > 0, 1.0, 0.0)
             even_ref[pairs + pair] = jnp.where(left, here, there)
-            odd_ref[pairs + pair] = jnp.where(left, h_swap[before] * started, here)
-            back_ref[pairs + pair] = jnp.where(left, there, h_spec[before] * started)
+            odd_ref[pairs + pair] = jnp.where(left, swapped[before] * started, here)
+            back_ref[pairs + pair] = jnp.where(left, there, spec[before] * started)
             return carry
 
         lax.fori_loop(0, pairs, one, 0)
@@ -405,45 +429,24 @@
 
         lax.fori_loop(0, rows // 8, one, 0)
 
-    def invert(unit, forward):
-        def one(step, carry):
-            block = jnp.concatenate([z_spec[2 * step], z_spec[2 * step + 1]], 1)
-            field = split_dot(inv_ref[...], block)
-            fields[2 * step + 1] = field[:, :128]
-            fields[2 * step + 2] = field[:, 128:]
-            return carry
-
-        lax.fori_loop(0, pairs // 2, one, 0)
-
-        def join(tile, carry):
-            left = first_lanes(rows)
-            here = swap(fields[tile + 1, rows:, :])
-            if forward:
-                there = swap(fields[tile, rows:, :])
-                result = fields[tile + 1, :rows, :] + jnp.where(left, there, here)
-            else:
-                there = swap(fields[tile + 2, rows:, :])
-                result = fields[tile + 1, :rows, :] - jnp.where(left, here, there)
-            pack(unit, tile, result)
-            return carry
-
-        lax.fori_loop(0, pairs, join, 0)
-
-    def pack_inputs(tile, carry):
+    def invert(pair):
+        return split_dot(inv_ref[...], z_spec[pair])
+
+    def pack_filter(tile, carry):
+        pack(FILTER, tile, f_ref[:, lanes(tile)])
+        return carry
+
+    def make_gated(tile):
         at = lanes(tile)
-        pack(FILTER, tile, f_ref[:, at])
-        pack(GATED, tile, k_ref[:, at].astype(f32) * v_ref[:, at].astype(f32))
-        return carry
-
-    for copy in loads[:3]:
+        return k_ref[:, at].astype(f32) * v_ref[:, at].astype(f32)
+
+    loads[0].wait()
+    lax.fori_loop(0, pairs, pack_filter, 0)
+    pl.semaphore_wait(barrier, seq_count)
+    send_tiles(FILTER, None)
+    for copy in loads[1:3]:
         copy.wait()
-    lax.fori_loop(0, pairs, pack_inputs, 0)
-    fields[0] = jnp.zeros((2 * rows, 128), f32)
-    fields[pairs + 1] = jnp.zeros((2 * rows, 128), f32)
-
-    pl.semaphore_wait(barrier, seq_count)
-    send_all(FILTER)
-    send_all(GATED)
+    send_tiles(GATED, make_gated)
     for copy in loads[3:]:
         copy.wait()
     clear_sums()
@@ -453,7 +456,8 @@
         return carry
 
     receive_each(FILTER, take_filter, 0)
-    lay_out_filter()
+    add_before(h_spec, h_swap, m_spec, m_swap)
+    lay_out(m_spec, m_swap)
 
     def take_gated(pair, carry):
         transform(GATED, x_spec, x_swap, pair)
@@ -461,9 +465,11 @@
         return carry
 
     receive_each(GATED, take_gated, 0)
-    invert(CONV, True)
-    send_all(CONV)
+    send_tiles(CONV, invert)
     clear_sums()
+    add_before(x_spec, x_swap, h_spec, h_swap)
+    sent_all(FILTER)
+    sent_all(GATED)
 
     def activate(tile, carry):
         squares, crosses = carry
@@ -477,8 +483,12 @@
 
     nothing = jnp.zeros((rows, 128), f32)
     squares, crosses = receive_each(CONV, activate, (nothing, nothing))
-    stat_send[0] = jnp.broadcast_to(jnp.sum(squares, axis=1, keepdims=True), (rows, 128))
-    stat_send[1] = jnp.broadcast_to(jnp.sum(crosses, axis=1, keepdims=True), (rows, 128))
+    left = first_lanes(rows)
+    stat_send[...] = jnp.where(
+        left,
+        jnp.broadcast_to(jnp.sum(squares, axis=1, keepdims=True), (rows, 128)),
+        jnp.broadcast_to(jnp.sum(crosses, axis=1, keepdims=True), (rows, 128)),
+    )
     stats = pltpu.make_async_remote_copy(
         src_ref=stat_send,
         dst_ref=stat_recv,
@@ -489,22 +499,22 @@
     )
     stats.start()
     stats.wait()
-    inverse_rms = lax.rsqrt((stat_send[0] + stat_recv[0]) / channel_total + epsilon_value)
-    cross_mean = (stat_send[1] + stat_recv[1]) / channel_total
+    means = (stat_send[...] + stat_recv[...]) / channel_total
+    other = swap(means)
+    inverse_rms = lax.rsqrt(jnp.where(left, means, other) + epsilon_value)
+    cross_mean = jnp.where(left, other, means)
     cubed = inverse_rms * inverse_rms * inverse_rms * cross_mean
 
-    def differentiate(tile, carry):
+    def differentiate(tile):
         at = lanes(tile)
         queries = q_ref[:, at].astype(f32)
         activated = queries * mixed_ref[tile]
         scaled = g_ref[:, at].astype(f32) * norm_ref[:, at]
         mix_grad = (inverse_rms * scaled - activated * cubed) * queries
         mix_ref[tile] = mix_grad
-        pack(MIXGRAD, tile, mix_grad)
-        return carry
-
-    lax.fori_loop(0, pairs, differentiate, 0)
-    send_all(MIXGRAD)
+        return mix_grad
+
+    send_tiles(MIXGRAD, differentiate)
 
     def first_outputs(tile, carry):
         at = lanes(tile)
@@ -518,6 +528,7 @@
     lax.fori_loop(0, pairs, first_outputs, 0)
     for copy in stores[:2]:
         copy.start()
+    sent_all(CONV)
 
     def take_grad(pair, carry):
         transform(MIXGRAD, m_spec, m_swap, pair)
@@ -525,11 +536,10 @@
         return carry
 
     receive_each(MIXGRAD, take_grad, 0)
-    invert(INPUT, False)
-    send_all(INPUT)
-    correlate(x_spec, x_swap)
-    invert(FGRAD, False)
-    send_all(FGRAD)
+    send_tiles(INPUT, invert)
+    correlate(h_spec, h_swap)
+    send_tiles(FGRAD, invert)
+    sent_all(MIXGRAD)
     def input_outputs(tile, carry):
         at = lanes(tile)
         gated_grad = unpack(INPUT, tile) + skip_ref[:, at] * mix_ref[tile]
@@ -540,6 +550,7 @@
     receive_each(INPUT, input_outputs, 0)
     for copy in stores[2:4]:
         copy.start()
+    sent_all(INPUT)
 
     def filter_outputs(tile, carry):
         fg_ref[:, lanes(tile)] = unpack(FGRAD, tile)
@@ -547,8 +558,7 @@
 
     receive_each(FGRAD, filter_outputs, 0)
     stores[4].start()
-    for unit in range(6):
-        sent_all(unit)
+    sent_all(FGRAD)
     for copy in stores:
         copy.wait()
 
@@ -587,7 +597,7 @@
     laid = pltpu.VMEM((2 * pairs, 2 * rows, 128), jnp.float32)
     blocks = pltpu.VMEM((6, seq_count, rows // 2, 128), jnp.float32)
     held = pltpu.VMEM((pairs, rows, 128), jnp.float32)
-    stat = pltpu.VMEM((2, rows, 128), jnp.float32)
+    stat = pltpu.VMEM((rows, 128), jnp.float32)
     narrow = jax.ShapeDtypeStruct((rows, width), jnp.bfloat16)
     shapes = (narrow,) * 4 + (jax.ShapeDtypeStruct((rows, width), jnp.float32),)
     results = pl.pallas_call(
@@ -597,7 +607,6 @@
         out_specs=(anywhere,) * 5,
         scratch_shapes=[pltpu.VMEM(one.shape, one.dtype) for one in shapes + operands] + [
             blocks, blocks, spec, spec, spec, spec, spec, spec, spec,
-            pltpu.VMEM((pairs + 2, 2 * rows, 128), jnp.float32),
             laid, laid, laid,
             held, held, stat, stat,
             pltpu.SemaphoreType.DMA((6, seq_count)),

time: 97.8 us -> 91.5 us (0.936)
  Pallas kernels: 97 us -> 90.6 us
    pallas_call x1, Pallas kernels: 94.7 us -> 88.4 us  [fast_body(): pl.pallas_call(functools.partial(fast_kernel, seq_count), out_shape=shape...]
where the time goes in v4:
time: 91.5 us; the launch traced here: 91.3 us
  Pallas kernels  90.6 us (99%)
    pallas_call x1, Pallas kernels, fast_body(): pl.pallas_call(functools.partial(fast_kernel, seq_count), out_shape=shape...  88.4 us
    pallas_call x1, Pallas kernels, fast_body(): pl.pallas_call(functools.partial(write_kernel, len(shapes)), out_shape=sh...  2.24 us

profile of v4, /device:TPU:8, one launch (start us, length us, event | category | flops | bytes accessed | tf_op | source)
XLA Modules:
  0.0 91.3 jit_solution(5745517464607514432)
XLA Ops:
  0.6 88.4 %shard_map.128 = (bf16[128,1024]{1,0:T(8,128)(2,1)}, bf16[128,1024]{1,0:T(8,128)(2,1)}, bf16[128,1024]{1,0:T(8,128)(2,1)}, bf16[128,1024]{1,0:T(8,128)(2,1)}, f32[128,1024]{1,0:T(8,128)}) custom-call(bf16[128,1024]{1,0:T(8,128)(2,1)} %q_hbm.1, bf16[128,1024]{1,0:T(8,128)(2,1)} %k_hbm.1, bf16[128,1024]{1,0:T(8,128)(2,1)} %v_hbm.1, f32[128,1024]{1,0:T(8,128)} %f_hbm.1, ...), custom_call_target="tpu_custom_call" | custom-call | flops 2000000000 | bytes 4000000 | tf_op jit(solution)/shard_map/pallas_call | solution.py:603
  89.0 2.2 %shard_map.129 = (bf16[128,1024]{1,0:T(8,128)(2,1)}, bf16[128,1024]{1,0:T(8,128)(2,1)}, bf16[128,1024]{1,0:T(8,128)(2,1)}, bf16[128,1024]{1,0:T(8,128)(2,1)}, f32[128,1024]{1,0:T(8,128)}) custom-call(bf16[128,1024]{1,0:T(8,128)(2,1)} %get-tuple-element.10.refs_0_, bf16[128,1024]{1,0:T(8,128)(2,1)} %get-tuple-element.11.refs_1_, ...), custom_call_target="tpu_custom_call" | custom-call | tf_op jit(solution)/shard_map/pallas_call | solution.py:625

commit v5 on v4

--- a/solution.py
+++ b/solution.py
@@ -279,7 +279,7 @@
 
         return pair
 
-    def send_tiles(unit, make):
+    def send_tiles(unit, make, first=0, last=pairs):
         def one(step, carry):
             flips = send_flips(step)
             if make is not None:
@@ -293,9 +293,9 @@
 
             return carry
 
-        lax.fori_loop(0, pairs, one, 0)
-
-    def receive_each(unit, use, carry):
+        lax.fori_loop(first, last, one, 0)
+
+    def receive_each(unit, use, carry, first=0, last=pairs):
         def one(step, carry):
             pair = for_peers(
                 receive_flips(step),
@@ -303,9 +303,9 @@
             )
             return use(pair, carry)
 
-        return lax.fori_loop(0, pairs, one, carry)
-
-    def sent_all(unit):
+        return lax.fori_loop(first, last, one, carry)
+
+    def sent_all(unit, first=0, last=pairs):
         def one(step, carry):
             for_peers(
                 send_flips(step),
@@ -313,7 +313,7 @@
             )
             return carry
 
-        lax.fori_loop(0, pairs, one, 0)
+        lax.fori_loop(first, last, one, 0)
 
     def transform(unit, spec, swapped, pair):
         field = split_dot(fwd_ref[...], unpack(unit, pair))
@@ -446,7 +446,7 @@
     send_tiles(FILTER, None)
     for copy in loads[1:3]:
         copy.wait()
-    send_tiles(GATED, make_gated)
+    send_tiles(GATED, make_gated, 0, pairs // 2)
     for copy in loads[3:]:
         copy.wait()
     clear_sums()
@@ -455,7 +455,9 @@
         transform(FILTER, h_spec, h_swap, pair)
         return carry
 
-    receive_each(FILTER, take_filter, 0)
+    receive_each(FILTER, take_filter, 0, 0, pairs // 2)
+    send_tiles(GATED, make_gated, pairs // 2)
+    receive_each(FILTER, take_filter, 0, pairs // 2)
     add_before(h_spec, h_swap, m_spec, m_swap)
     lay_out(m_spec, m_swap)
 
@@ -514,7 +516,7 @@
         mix_ref[tile] = mix_grad
         return mix_grad
 
-    send_tiles(MIXGRAD, differentiate)
+    send_tiles(MIXGRAD, differentiate, 0, pairs // 2)
 
     def first_outputs(tile, carry):
         at = lanes(tile)
@@ -529,6 +531,8 @@
     for copy in stores[:2]:
         copy.start()
     sent_all(CONV)
+    sent_all(MIXGRAD, 0, pairs // 4)
+    send_tiles(MIXGRAD, differentiate, pairs // 2)
 
     def take_grad(pair, carry):
         transform(MIXGRAD, m_spec, m_swap, pair)
@@ -539,7 +543,7 @@
     send_tiles(INPUT, invert)
     correlate(h_spec, h_swap)
     send_tiles(FGRAD, invert)
-    sent_all(MIXGRAD)
+    sent_all(MIXGRAD, pairs // 4)
     def input_outputs(tile, carry):
         at = lanes(tile)
         gated_grad = unpack(INPUT, tile) + skip_ref[:, at] * mix_ref[tile]

time: 91.5 us -> 91.6 us (level)
  no operation moved by 1% of the time
where the time goes in v5:
time: 91.6 us; the launch traced here: 91.4 us
  Pallas kernels  90.8 us (99%)
    pallas_call x1, Pallas kernels, fast_body(): pl.pallas_call(functools.partial(fast_kernel, seq_count), out_shape=shape...  88.5 us
    pallas_call x1, Pallas kernels, fast_body(): pl.pallas_call(functools.partial(write_kernel, len(shapes)), out_shape=sh...  2.24 us

profile of v5, /device:TPU:8, one launch (start us, length us, event | category | flops | bytes accessed | tf_op | source)
XLA Modules:
  0.0 91.4 jit_solution(10405337307306080647)
XLA Ops:
  0.6 88.5 %shard_map.128 = (bf16[128,1024]{1,0:T(8,128)(2,1)}, bf16[128,1024]{1,0:T(8,128)(2,1)}, bf16[128,1024]{1,0:T(8,128)(2,1)}, bf16[128,1024]{1,0:T(8,128)(2,1)}, f32[128,1024]{1,0:T(8,128)}) custom-call(bf16[128,1024]{1,0:T(8,128)(2,1)} %q_hbm.1, bf16[128,1024]{1,0:T(8,128)(2,1)} %k_hbm.1, bf16[128,1024]{1,0:T(8,128)(2,1)} %v_hbm.1, f32[128,1024]{1,0:T(8,128)} %f_hbm.1, ...), custom_call_target="tpu_custom_call" | custom-call | flops 2000000000 | bytes 4000000 | tf_op jit(solution)/shard_map/pallas_call | solution.py:607
  89.2 2.2 %shard_map.129 = (bf16[128,1024]{1,0:T(8,128)(2,1)}, bf16[128,1024]{1,0:T(8,128)(2,1)}, bf16[128,1024]{1,0:T(8,128)(2,1)}, bf16[128,1024]{1,0:T(8,128)(2,1)}, f32[128,1024]{1,0:T(8,128)}) custom-call(bf16[128,1024]{1,0:T(8,128)(2,1)} %get-tuple-element.10.refs_0_, bf16[128,1024]{1,0:T(8,128)(2,1)} %get-tuple-element.11.refs_1_, ...), custom_call_target="tpu_custom_call" | custom-call | tf_op jit(solution)/shard_map/pallas_call | solution.py:629

commit v6 on v5

--- a/solution.py
+++ b/solution.py
@@ -350,44 +350,45 @@
     def lay_out(spec, swapped):
         def one(pair, carry):
             left = first_lanes(2 * rows)
-            nothing = jnp.zeros((2 * rows, 128), f32)
-            even_ref[pair] = nothing
-            odd_ref[pair] = nothing
-            back_ref[pair] = nothing
             here, there = spec[pair], swapped[pair]
             before = lax.rem(pair + pairs - 1, pairs)
             started = jnp.where(pair > 0, 1.0, 0.0)
-            even_ref[pairs + pair] = jnp.where(left, here, there)
-            odd_ref[pairs + pair] = jnp.where(left, swapped[before] * started, here)
-            back_ref[pairs + pair] = jnp.where(left, there, spec[before] * started)
+            even_ref[pair] = jnp.where(left, here, there)
+            odd_ref[pair] = jnp.where(left, swapped[before] * started, here)
+            back_ref[pair] = jnp.where(left, there, spec[before] * started)
             return carry
 
         lax.fori_loop(0, pairs, one, 0)
 
     def add_products(spec, swapped, pair, forward):
-        def one(tile, carry):
-            first = pl.multiple_of(tile * 8, 8)
-            real_rows, imag_rows = pl.ds(first, 8), pl.ds(first + rows, 8)
-            xr, xi = spec[pair, real_rows, :], spec[pair, imag_rows, :]
-            yr, yi = swapped[pair, real_rows, :], swapped[pair, imag_rows, :]
-            for n in range(pairs):
-                if forward:
-                    place, cross = pairs + n - pair, odd_ref
-                else:
-                    place, cross = pairs + pair - n, back_ref
-                er, ei = even_ref[place, real_rows, :], even_ref[place, imag_rows, :]
-                tr, ti = cross[place, real_rows, :], cross[place, imag_rows, :]
-                if forward:
-                    real = (xr * er - xi * ei) + (yr * tr - yi * ti)
-                    imag = (xr * ei + xi * er) + (yr * ti + yi * tr)
-                else:
-                    real = (xr * er + xi * ei) + (yr * tr + yi * ti)
-                    imag = (xi * er - xr * ei) + (yi * tr - yr * ti)
-                z_spec[n, real_rows, :] = z_spec[n, real_rows, :] + real
-                z_spec[n, imag_rows, :] = z_spec[n, imag_rows, :] + imag
-            return carry
-
-        lax.fori_loop(0, rows // 8, one, 0)
+        def one(n, carry):
+            place = n - pair if forward else pair - n
+            cross = odd_ref if forward else back_ref
+
+            def some(group, carry):
+                for part in range(4):
+                    first = pl.multiple_of(group * 32 + part * 8, 8)
+                    real_rows, imag_rows = pl.ds(first, 8), pl.ds(first + rows, 8)
+                    xr, xi = spec[pair, real_rows, :], spec[pair, imag_rows, :]
+                    yr, yi = swapped[pair, real_rows, :], swapped[pair, imag_rows, :]
+                    er, ei = even_ref[place, real_rows, :], even_ref[place, imag_rows, :]
+                    tr, ti = cross[place, real_rows, :], cross[place, imag_rows, :]
+                    if forward:
+                        real = (xr * er - xi * ei) + (yr * tr - yi * ti)
+                        imag = (xr * ei + xi * er) + (yr * ti + yi * tr)
+                    else:
+                        real = (xr * er + xi * ei) + (yr * tr + yi * ti)
+                        imag = (xi * er - xr * ei) + (yi * tr - yr * ti)
+                    z_spec[n, real_rows, :] = z_spec[n, real_rows, :] + real
+                    z_spec[n, imag_rows, :] = z_spec[n, imag_rows, :] + imag
+                return carry
+
+            return lax.fori_loop(0, rows // 32, some, carry)
+
+        if forward:
+            lax.fori_loop(pair, pairs, one, 0)
+        else:
+            lax.fori_loop(0, pair + 1, one, 0)
 
     def load(ref, tile, count):
         first = pl.multiple_of(tile * 8, 8)
@@ -598,7 +599,6 @@
     )
     anywhere = pl.BlockSpec(memory_space=pltpu.HBM)
     spec = pltpu.VMEM((pairs, 2 * rows, 128), jnp.float32)
-    laid = pltpu.VMEM((2 * pairs, 2 * rows, 128), jnp.float32)
     blocks = pltpu.VMEM((6, seq_count, rows // 2, 128), jnp.float32)
     held = pltpu.VMEM((pairs, rows, 128), jnp.float32)
     stat = pltpu.VMEM((rows, 128), jnp.float32)
@@ -611,7 +611,7 @@
         out_specs=(anywhere,) * 5,
         scratch_shapes=[pltpu.VMEM(one.shape, one.dtype) for one in shapes + operands] + [
             blocks, blocks, spec, spec, spec, spec, spec, spec, spec,
-            laid, laid, laid,
+            spec, spec, spec,
             held, held, stat, stat,
             pltpu.SemaphoreType.DMA((6, seq_count)),
             pltpu.SemaphoreType.DMA((6, seq_count)),

time: 91.6 us -> 88.6 us (0.967)
  Pallas kernels: 90.8 us -> 87.8 us
    pallas_call x1, Pallas kernels: 88.5 us -> 85.5 us  [fast_body(): pl.pallas_call(functools.partial(fast_kernel, seq_count), out_shape=shape...]
where the time goes in v6:
time: 88.6 us; the launch traced here: 88.4 us
  Pallas kernels  87.8 us (99%)
    pallas_call x1, Pallas kernels, fast_body(): pl.pallas_call(functools.partial(fast_kernel, seq_count), out_shape=shape...  85.5 us
    pallas_call x1, Pallas kernels, fast_body(): pl.pallas_call(functools.partial(write_kernel, len(shapes)), out_shape=sh...  2.24 us

profile of v6, /device:TPU:8, one launch (start us, length us, event | category | flops | bytes accessed | tf_op | source)
XLA Modules:
  0.0 88.4 jit_solution(1783422704105972486)
XLA Ops:
  0.6 85.5 %shard_map.128 = (bf16[128,1024]{1,0:T(8,128)(2,1)}, bf16[128,1024]{1,0:T(8,128)(2,1)}, bf16[128,1024]{1,0:T(8,128)(2,1)}, bf16[128,1024]{1,0:T(8,128)(2,1)}, f32[128,1024]{1,0:T(8,128)}) custom-call(bf16[128,1024]{1,0:T(8,128)(2,1)} %q_hbm.1, bf16[128,1024]{1,0:T(8,128)(2,1)} %k_hbm.1, bf16[128,1024]{1,0:T(8,128)(2,1)} %v_hbm.1, f32[128,1024]{1,0:T(8,128)} %f_hbm.1, ...), custom_call_target="tpu_custom_call" | custom-call | flops 2000000000 | bytes 4000000 | tf_op jit(solution)/shard_map/pallas_call | solution.py:607
  86.2 2.2 %shard_map.129 = (bf16[128,1024]{1,0:T(8,128)(2,1)}, bf16[128,1024]{1,0:T(8,128)(2,1)}, bf16[128,1024]{1,0:T(8,128)(2,1)}, bf16[128,1024]{1,0:T(8,128)(2,1)}, f32[128,1024]{1,0:T(8,128)}) custom-call(bf16[128,1024]{1,0:T(8,128)(2,1)} %get-tuple-element.10.refs_0_, bf16[128,1024]{1,0:T(8,128)(2,1)} %get-tuple-element.11.refs_1_, ...), custom_call_target="tpu_custom_call" | custom-call | tf_op jit(solution)/shard_map/pallas_call | solution.py:629

commit v7 on v6

--- a/solution.py
+++ b/solution.py
@@ -361,16 +361,24 @@
         lax.fori_loop(0, pairs, one, 0)
 
     def add_products(spec, swapped, pair, forward):
-        def one(n, carry):
-            place = n - pair if forward else pair - n
-            cross = odd_ref if forward else back_ref
-
-            def some(group, carry):
-                for part in range(4):
-                    first = pl.multiple_of(group * 32 + part * 8, 8)
-                    real_rows, imag_rows = pl.ds(first, 8), pl.ds(first + rows, 8)
-                    xr, xi = spec[pair, real_rows, :], spec[pair, imag_rows, :]
-                    yr, yi = swapped[pair, real_rows, :], swapped[pair, imag_rows, :]
+        cross = odd_ref if forward else back_ref
+
+        def some(group, carry):
+            places = []
+            for part in range(8):
+                first = pl.multiple_of(group * 64 + part * 8, 8)
+                places.append((pl.ds(first, 8), pl.ds(first + rows, 8)))
+            held = [
+                (
+                    spec[pair, real_rows, :], spec[pair, imag_rows, :],
+                    swapped[pair, real_rows, :], swapped[pair, imag_rows, :],
+                )
+                for real_rows, imag_rows in places
+            ]
+
+            def one(n, carry):
+                place = n - pair if forward else pair - n
+                for (real_rows, imag_rows), (xr, xi, yr, yi) in zip(places, held):
                     er, ei = even_ref[place, real_rows, :], even_ref[place, imag_rows, :]
                     tr, ti = cross[place, real_rows, :], cross[place, imag_rows, :]
                     if forward:
@@ -383,12 +391,11 @@
                     z_spec[n, imag_rows, :] = z_spec[n, imag_rows, :] + imag
                 return carry
 
-            return lax.fori_loop(0, rows // 32, some, carry)
-
-        if forward:
-            lax.fori_loop(pair, pairs, one, 0)
-        else:
-            lax.fori_loop(0, pair + 1, one, 0)
+            if forward:
+                return lax.fori_loop(pair, pairs, one, carry)
+            return lax.fori_loop(0, pair + 1, one, carry)
+
+        lax.fori_loop(0, rows // 64, some, 0)
 
     def load(ref, tile, count):
         first = pl.multiple_of(tile * 8, 8)

time: 88.6 us -> 87.5 us (0.988)
  Pallas kernels: 87.8 us -> 86.5 us
    pallas_call x1, Pallas kernels: 85.5 us -> 84.3 us  [fast_body(): pl.pallas_call(functools.partial(fast_kernel, seq_count), out_shape=shape...]
where the time goes in v7:
time: 87.5 us; the launch traced here: 87.1 us
  Pallas kernels  86.5 us (99%)
    pallas_call x1, Pallas kernels, fast_body(): pl.pallas_call(functools.partial(fast_kernel, seq_count), out_shape=shape...  84.3 us
    pallas_call x1, Pallas kernels, fast_body(): pl.pallas_call(functools.partial(write_kernel, len(shapes)), out_shape=sh...  2.24 us

profile of v7, /device:TPU:8, one launch (start us, length us, event | category | flops | bytes accessed | tf_op | source)
XLA Modules:
  0.0 87.1 jit_solution(2230484438495682532)
XLA Ops:
  0.6 84.3 %shard_map.128 = (bf16[128,1024]{1,0:T(8,128)(2,1)}, bf16[128,1024]{1,0:T(8,128)(2,1)}, bf16[128,1024]{1,0:T(8,128)(2,1)}, bf16[128,1024]{1,0:T(8,128)(2,1)}, f32[128,1024]{1,0:T(8,128)}) custom-call(bf16[128,1024]{1,0:T(8,128)(2,1)} %q_hbm.1, bf16[128,1024]{1,0:T(8,128)(2,1)} %k_hbm.1, bf16[128,1024]{1,0:T(8,128)(2,1)} %v_hbm.1, f32[128,1024]{1,0:T(8,128)} %f_hbm.1, ...), custom_call_target="tpu_custom_call" | custom-call | flops 2000000000 | bytes 4000000 | tf_op jit(solution)/shard_map/pallas_call | solution.py:614
  84.9 2.2 %shard_map.129 = (bf16[128,1024]{1,0:T(8,128)(2,1)}, bf16[128,1024]{1,0:T(8,128)(2,1)}, bf16[128,1024]{1,0:T(8,128)(2,1)}, bf16[128,1024]{1,0:T(8,128)(2,1)}, f32[128,1024]{1,0:T(8,128)}) custom-call(bf16[128,1024]{1,0:T(8,128)(2,1)} %get-tuple-element.10.refs_0_, bf16[128,1024]{1,0:T(8,128)(2,1)} %get-tuple-element.11.refs_1_, ...), custom_call_target="tpu_custom_call" | custom-call | tf_op jit(solution)/shard_map/pallas_call | solution.py:636
